TPU v7x, 32 devices: a whole 2x2x4 slice. The times are simulated.
32 devices in a mesh: seq: 8 (over y, x, core), chan: 4 (over z).
Axes of the slice: x: 2, y: 2, z: 4, core: 2. Of those that a mesh axis runs over, the one named last changes fastest.
Arguments:
- hyena_query: bfloat16 [2048, 8192], P('seq', 'chan'), may hold values from -6 to 6
- hyena_key: bfloat16 [2048, 8192], P('seq', 'chan'), may hold values from -6 to 6
- hyena_value: bfloat16 [2048, 8192], P('seq', 'chan'), may hold values from -6 to 6
- bias: float32 [8192], P('chan'), may hold values from 0.5 to 1.5
- groups: int32 [8192], P('chan'), may hold values from 0 to 511
- filters: float32 [512, 2048], P('chan', 'seq'), may hold values from -1.5 to 1.5
- att_queries: bfloat16 [2048, 8192], P('seq', 'chan'), may hold values from -45 to 45
- att_keys: bfloat16 [2048, 8192], P('seq', 'chan'), may hold values from -5 to 5
- block_mask: int32 [16, 16], P('seq'), may hold values from 0 to 1, as said below
Outputs:
- hyena_out: bfloat16 [2048, 8192], P('seq', 'chan')
- attn_out: bfloat16 [2048, 8192], P('seq', 'chan')
Inputs may be any that keep to these rules, and one draw needn't show every extreme that they name: block_mask[i, i] = 1 and block_mask[i, j] = 0 for j > i.
All inputs are finite; a program needn't handle non-finite values.
Results may differ from a plain program's by a relative error of at most 0.014.
Values may be sent and summed in bfloat16 or wider, within the bound.
A program may use at most 128 MiB of HBM per device.

v0:
```python
import math

import jax
import jax.numpy as jnp
from jax import lax
from jax.sharding import PartitionSpec as P

HD = 128
ABLK = 128


highest = lax.Precision.HIGHEST


def swapped(value, axis, stride):
    mask = 2**stride
    pairs = [(source, source ^ mask) for source in range(lax.axis_size(axis))]
    return lax.ppermute(value, axis, pairs)


def shortened(x):

    def short(part):
        return part.astype(jnp.bfloat16) if part.dtype == jnp.float32 else part

    return jax.tree.map(short, x)


def unit_angle(numer, denom):
    return 2.0 * math.pi / denom * numer.astype(jnp.float32)


def twist(real_part, imag_part, cosine, sine):
    return (real_part * cosine - imag_part * sine, real_part * sine + imag_part * cosine)


def expand_pair(signal, device, rows_dev, length):
    positions = device * rows_dev + jnp.arange(rows_dev, dtype=jnp.int32)
    angles = math.pi / length * positions.astype(jnp.float32)
    values = signal.astype(jnp.float32)
    cosine = jnp.cos(angles)[:, None]
    sine = jnp.sin(angles)[:, None]
    real_part = jnp.stack([values, values * cosine])
    imag_part = jnp.stack([jnp.zeros_like(values), -values * sine])
    return (real_part, imag_part)


def section_twiddle(device, level, rows_dev, sign):
    inner = device % (1 << level) * rows_dev + jnp.arange(rows_dev, dtype=jnp.int32)
    angles = unit_angle(inner, rows_dev << level + 1)
    return (jnp.cos(angles)[:, None], sign * jnp.sin(angles)[:, None])


def forward_section(current, partner, device, level, rows_dev):
    cosine, sine = section_twiddle(device, level, rows_dev, -1.0)
    upper = device >> level & 1 == 1
    diff_re = partner[0] - current[0]
    diff_im = partner[1] - current[1]
    turned_re, turned_im = twist(diff_re, diff_im, cosine, sine)
    return (
        jnp.where(upper, turned_re, current[0] + partner[0]),
        jnp.where(upper, turned_im, current[1] + partner[1]),
    )


def inverse_section(current, partner, device, level, rows_dev):
    cosine, sine = section_twiddle(device, level, rows_dev, 1.0)
    upper = device >> level & 1 == 1
    moved_re = jnp.where(upper, current[0], partner[0])
    moved_im = jnp.where(upper, current[1], partner[1])
    base_re = jnp.where(upper, partner[0], current[0])
    base_im = jnp.where(upper, partner[1], current[1])
    turned_re, turned_im = twist(moved_re, moved_im, cosine, sine)
    factor = jnp.where(upper, -1.0, 1.0)
    return (base_re + factor * turned_re, base_im + factor * turned_im)


def local_dft(real_part, imag_part, rows_dev, sign):
    index = jnp.arange(rows_dev, dtype=jnp.int32)
    angles = unit_angle(index[:, None] * index[None, :] % rows_dev, rows_dev)
    cosine = jnp.cos(angles)
    sine = sign * jnp.sin(angles)

    def apply_matrix(matrix, data):
        return jnp.einsum("km,emc->ekc", matrix, data, precision=highest)

    new_re = apply_matrix(cosine, real_part) - apply_matrix(sine, imag_part)
    new_im = apply_matrix(cosine, imag_part) + apply_matrix(sine, real_part)
    return (new_re, new_im)


def butterfly_conv(mixed, bank, groups):
    rows_dev, channels = mixed.shape
    devices = lax.axis_size("seq")
    length = rows_dev * devices
    bit_count = devices.bit_length() - 1
    device = lax.axis_index("seq")
    top_level = bit_count - 1
    partner_mixed = swapped(mixed, "seq", top_level)
    current = expand_pair(mixed, device, rows_dev, length)
    partner = expand_pair(partner_mixed, jnp.bitwise_xor(device, 1 << top_level), rows_dev, length)
    state = forward_section(current, partner, device, top_level, rows_dev)
    for level in range(top_level - 1, -1, -1):
        received = swapped(shortened(jnp.stack(state)), "seq", level)
        state = forward_section(state, (received[0], received[1]), device, level, rows_dev)
    spec_re, spec_im = local_dft(state[0], state[1], rows_dev, -1.0)
    residue = jnp.zeros((), jnp.int32)
    for level in range(bit_count):
        residue = residue + ((device >> level & 1) << bit_count - 1 - level)
    freq_even = 2 * (residue + devices * jnp.arange(rows_dev, dtype=jnp.int32))
    freqs = jnp.concatenate([freq_even, freq_even + 1])
    lags = jnp.arange(length, dtype=jnp.int32)
    angles = unit_angle(lags[:, None] * freqs[None, :] % (2 * length), 2 * length)
    table_re = jnp.dot(bank, jnp.cos(angles), precision=highest)
    table_im = -jnp.dot(bank, jnp.sin(angles), precision=highest)
    chosen_re = jnp.take(table_re, groups, axis=0).T.reshape(2, rows_dev, channels)
    chosen_im = jnp.take(table_im, groups, axis=0).T.reshape(2, rows_dev, channels)
    prod_re, prod_im = twist(spec_re, spec_im, chosen_re, chosen_im)
    state = local_dft(prod_re, prod_im, rows_dev, 1.0)
    for level in range(bit_count):
        received = swapped(shortened(jnp.stack(state)), "seq", level)
        state = inverse_section(state, (received[0], received[1]), device, level, rows_dev)
    positions = device * rows_dev + jnp.arange(rows_dev, dtype=jnp.int32)
    final_angles = math.pi / length * positions.astype(jnp.float32)
    cosine = jnp.cos(final_angles)[:, None]
    sine = jnp.sin(final_angles)[:, None]
    return (state[0][0] + cosine * state[0][1] - sine * state[1][1]) / (2.0 * length)


def attention(att_queries, att_keys, hyena_out, block_mask):
    rows_dev, channels = att_queries.shape
    head_count = channels // HD
    device = lax.axis_index("seq")
    block_count = block_mask.shape[1]
    queries = att_queries.reshape(rows_dev, head_count, HD)
    mask_rows = jnp.repeat(block_mask, ABLK, axis=0).astype(jnp.float32)
    query_pos = device * rows_dev + jnp.arange(rows_dev, dtype=jnp.int32)
    scale = HD ** (-0.5)
    key_piece = lax.all_gather(att_keys, "seq", axis=0, tiled=True)
    value_piece = lax.all_gather(hyena_out, "seq", axis=0, tiled=True)
    piece_rows = key_piece.shape[0]
    key_pos = jnp.arange(piece_rows, dtype=jnp.int32)
    onehot = (
        jnp.arange(block_count, dtype=jnp.int32)[:, None] == (key_pos // ABLK)[None, :]
    ).astype(jnp.float32)
    allowed = (jnp.dot(mask_rows, onehot, preferred_element_type=jnp.float32) > 0.5) & (
        key_pos[None, :] <= query_pos[:, None]
    )
    keys_here = key_piece.reshape(piece_rows, head_count, HD)
    values_here = value_piece.reshape(piece_rows, head_count, HD)
    scores = (
        jnp.einsum("thd,shd->hts", queries, keys_here, preferred_element_type=jnp.float32) * scale
    )
    scores = jnp.where(allowed[None], scores, -1e30)
    old_max = jnp.full((head_count, rows_dev), -1e30, jnp.float32)
    new_max = jnp.maximum(old_max, jnp.max(scores, axis=-1))
    weights = jnp.where(allowed[None], jnp.exp(scores - new_max[..., None]), 0.0)
    new_total = jnp.sum(weights, axis=-1)
    new_acc = jnp.einsum(
        "hts,shd->htd",
        weights.astype(jnp.bfloat16),
        values_here,
        preferred_element_type=jnp.float32,
    )
    result = new_acc / new_total[..., None]
    return result.transpose(1, 0, 2).reshape(rows_dev, channels).astype(jnp.bfloat16)


def on_device(
    hyena_query, hyena_key, hyena_value, bias, groups, filters, att_queries, att_keys, block_mask
):
    mixed = (hyena_key.astype(jnp.float32) * hyena_value.astype(jnp.float32)).astype(jnp.bfloat16)
    bank = lax.all_gather(filters.astype(jnp.bfloat16), "chan", axis=0, tiled=True).astype(
        filters.dtype
    )
    bank = lax.all_gather(bank.astype(jnp.bfloat16), "seq", axis=1, tiled=True).astype(bank.dtype)
    conv = butterfly_conv(mixed, bank, groups)
    hyena_out = (
        hyena_query.astype(jnp.float32) * (conv + bias[None, :] * mixed.astype(jnp.float32))
    ).astype(jnp.bfloat16)
    attn_out = attention(att_queries, att_keys, hyena_out, block_mask)
    return (hyena_out, attn_out)


def solution(mesh):
    return jax.shard_map(
        on_device,
        mesh=mesh,
        in_specs=(
            P("seq", "chan"),
            P("seq", "chan"),
            P("seq", "chan"),
            P("chan"),
            P("chan"),
            P("chan", "seq"),
            P("seq", "chan"),
            P("seq", "chan"),
            P("seq", None),
        ),
        out_specs=(P("seq", "chan"), P("seq", "chan")),
        check_vma=False,
    )
```

profile of v0, /device:TPU:0, one launch (start us, length us, event | category | flops | bytes accessed | tf_op | source)
XLA Modules:
  0.0 638.1 jit_solution(7826261851672867493)
XLA Ops:
  7.3 1.5 copy.21
  8.8 2.3 copy.22
  11.1 3.0 fusion.36
  14.1 3.0 collective-permute-start
  17.2 0.2 convert_bitcast_fusion
  17.3 0.1 fusion.34
  17.5 22.7 %collective-permute-done = bf16[256,2048]{0,1:T(8,128)(2,1)S(1)} collective-permute-done((bf16[256,2048]{0,1:T(8,128)(2,1)S(1)}, bf16[256,2048]{0,1:T(8,128)(2,1)S(1)}, u32[]{:S(2)}, u32[]{:S(2)}) %collective-permute-start) | collective-permute-done | bytes 1048608 | tf_op jit(solution)/shard_map/ppermute | solution.py:18
  40.2 0.2 convert_bitcast_fusion.1
  40.4 0.3 fusion.31
  40.7 4.2 convert_bitcast_fusion.8
  44.9 2.3 pad_maximum_fusion.2
  47.2 1.7 collective-permute-start.1
  49.0 14.9 %all_gather.12 = bf16[512,256]{1,0:T(8,128)(2,1)} all-gather(bf16[128,256]{1,0:T(8,128)(2,1)S(1)} %convert_element_type.244), channel_id=1, replica_groups=mesh['seq'=8,'chan'=4] {'chan'}, dimensions={0}, use_global_device_ids=true | all-gather | bytes 327680 | tf_op jit(solution)/shard_map/all_gather | solution.py:173
  63.9 0.0 all-gather.6.cloned.1.call-start
  64.0 83.8 %collective-permute-done.1 = bf16[2,2,256,2048]{2,3,1,0:T(8,128)(2,1)} collective-permute-done((bf16[2,2,256,2048]{2,3,1,0:T(8,128)(2,1)}, bf16[2,2,256,2048]{2,3,1,0:T(8,128)(2,1)}, u32[]{:S(2)}, u32[]{:S(2)}) %collective-permute-start.1) | collective-permute-done | bytes 4194336 | tf_op jit(solution)/shard_map/ppermute | solution.py:18
  147.7 7.8 %convert_bitcast_fusion.6 = (bf16[1,2,256,2048]{2,3,1,0:T(8,128)(2,1)S(1)}, f32[2,256,2048]{1,2,0:T(8,128)}, bf16[1,2,256,2048]{2,3,1,0:T(8,128)(2,1)S(1)}, f32[2,256,2048]{1,2,0:T(8,128)}) fusion(f32[2,256,2048]{1,2,0:T(8,128)} %get-tuple-element.24, f32[256]{0:T(256)S(1)} %get-tuple-element.46, bf16[2,2,256,2048]{2,3,1,0:T(8,128)(2,1)} %collective-permute-done.1, ...), kind=kLoop, calls=%fused_computation.128 | loop fusion | flops 16777216 | bytes 25167872 | tf_op jit(solution)/shard_map/stack | solution.py:104
  155.5 2.3 pad_maximum_fusion.3
  158.0 23.5 %fusion.57 = f32[512,512]{0,1:T(8,128)S(1)} fusion(bf16[512,2048]{1,0:T(8,128)(2,1)} %all-gather.4.cloned.1.call-done, s32[512]{0:T(512)S(1)} %pad_add_fusion.1), kind=kOutput, calls=%fused_computation.134 | convolution fusion | flops 6457131008 | bytes 3147776 | tf_op jit(solution)/shard_map/dot_general | solution.py:114
  181.5 0.3 copy.23
  181.8 24.5 %fusion.63 = f32[512,512]{0,1:T(8,128)} fusion(bf16[512,2048]{1,0:T(8,128)(2,1)} %all-gather.4.cloned.1.call-done, s32[512]{0:T(512)S(1)} %pad_add_fusion.1), kind=kOutput, calls=%fused_computation.136 | convolution fusion | flops 6457393152 | bytes 3147776 | tf_op jit(solution)/shard_map/dot_general | solution.py:115
  206.3 1.6 copy.26
  207.8 8.9 %gather_fusion.1 = f32[2048,512]{1,0:T(8,128)} fusion(f32[512,512]{1,0:T(8,128)S(1)} %copy.26, s32[2048]{0:T(1024)S(1)} %fusion.107), kind=kCustom, calls=%fused_computation.1.clone | custom fusion | bytes 8396800 | tf_op jit(solution)/shard_map/jit(_take)/gather | solution.py:117
  216.8 9.4 %gather_fusion = f32[2048,512]{1,0:T(8,128)} fusion(f32[512,512]{1,0:T(8,128)S(1)} %copy.23, s32[2048]{0:T(1024)S(1)} %fusion.107), kind=kCustom, calls=%fused_computation.clone | custom fusion | bytes 8396800 | tf_op jit(solution)/shard_map/jit(_take)/gather | solution.py:116
  226.1 5.9 select_bitcast_fusion
  232.0 5.4 copy.27
  237.4 5.4 copy.28
  242.8 5.4 copy.24
  248.2 5.4 copy.25
  253.6 5.6 fusion.10
  259.2 4.4 fusion.76
  263.6 7.1 %fusion.74 = f32[2,2048,256]{2,1,0:T(8,128)} fusion(f32[2,256,2048]{1,2,0:T(8,128)S(1)} %get-tuple-element.34), kind=kOutput, calls=%fused_computation.148 | convolution fusion | flops 3222208512 | bytes 8388608 | tf_op jit(solution)/shard_map/km,emc->ekc/dot_general | solution.py:85
  270.8 4.6 convolution_subtract_fusion.1
  275.4 9.3 %fusion.19 = (f32[2,256,2048]{1,2,0:T(8,128)S(1)}, f32[2,256,2048]{1,2,0:T(8,128)S(1)}) fusion(f32[2,256,2048]{1,2,0:T(8,128)S(1)} %copy-done.4, f32[2,256,2048]{1,2,0:T(8,128)} %copy.25, f32[2,2048,256]{2,1,0:T(8,128)S(1)} %convolution_subtract_fusion.1, f32[2,2048,256]{2,1,0:T(8,128)} %fusion.74, f32[2,256,2048]{1,2,0:T(8,128)S(1)} %get-tuple-element.33), kind=kOutput, calls=%fused_computation.56 | convolution fusion | flops 3229483008 | bytes 29360128 | tf_op jit(solution)/shard_map/km,emc->ekc/dot_general | solution.py:85
  284.7 4.8 fusion.80
  289.5 4.4 fusion.78
  293.9 4.4 convolution_subtract_fusion
  298.4 4.8 convolution_add_fusion
  303.2 2.0 copy-done.2
  305.2 0.2 fusion.41
  305.4 0.2 fusion.40
  305.6 2.3 pad_maximum_fusion.4
  308.0 0.5 collective-permute-start.3
  308.5 1.3 copy.32
  309.9 5.7 collective-permute-done.3
  315.6 8.8 %convert_bitcast_fusion.5 = (bf16[1,2,256,2048]{2,3,1,0:T(8,128)(2,1)S(1)}, f32[2,256,2048]{1,2,0:T(8,128)}, bf16[1,2,256,2048]{2,3,1,0:T(8,128)(2,1)S(1)}, f32[2,256,2048]{1,2,0:T(8,128)}) fusion(f32[256]{0:T(256)S(1)} %fusion.108, bf16[2,2,256,2048]{2,3,1,0:T(8,128)(2,1)} %collective-permute-done.3, f32[2,2048,256]{2,1,0:T(8,128)} %copy-done.2, ...), kind=kLoop, calls=%fused_computation.127 | loop fusion | flops 18874368 | bytes 25167876 | tf_op jit(solution)/shard_map/stack | solution.py:121
  324.4 2.4 pad_maximum_fusion.5
  326.8 1.6 collective-permute-start.4
  328.4 116.8 %collective-permute-done.4 = bf16[2,2,256,2048]{2,3,1,0:T(8,128)(2,1)} collective-permute-done((bf16[2,2,256,2048]{2,3,1,0:T(8,128)(2,1)}, bf16[2,2,256,2048]{2,3,1,0:T(8,128)(2,1)}, u32[]{:S(2)}, u32[]{:S(2)}) %collective-permute-start.4) | collective-permute-done | bytes 4194336 | tf_op jit(solution)/shard_map/ppermute | solution.py:18
  445.3 7.9 %convert_bitcast_fusion.3 = (bf16[1,2,256,2048]{2,3,1,0:T(8,128)(2,1)S(1)}, f32[2,256,2048]{1,2,0:T(8,128)}, bf16[1,2,256,2048]{2,3,1,0:T(8,128)(2,1)S(1)}, f32[2,256,2048]{1,2,0:T(8,128)}) fusion(f32[256]{0:T(256)S(1)} %fusion.110, f32[2,256,2048]{1,2,0:T(8,128)} %get-tuple-element.32, bf16[2,2,256,2048]{2,3,1,0:T(8,128)(2,1)} %collective-permute-done.4, ...), kind=kLoop, calls=%fused_computation.125 | loop fusion | flops 18874368 | bytes 25167876 | tf_op jit(solution)/shard_map/stack | solution.py:121
  453.2 2.4 pad_maximum_fusion.6
  455.6 1.5 collective-permute-start.5
  457.1 0.5 copy.20
  457.6 90.6 %collective-permute-done.5 = bf16[2,2,256,2048]{2,3,1,0:T(8,128)(2,1)} collective-permute-done((bf16[2,2,256,2048]{2,3,1,0:T(8,128)(2,1)}, bf16[2,2,256,2048]{2,3,1,0:T(8,128)(2,1)}, u32[]{:S(2)}, u32[]{:S(2)}) %collective-permute-start.5) | collective-permute-done | bytes 4194336 | tf_op jit(solution)/shard_map/ppermute | solution.py:18
  548.3 1.9 fusion.51
  550.2 4.2 fusion.15
  554.5 2.1 fusion.39
  556.7 0.6 fusion.30
  557.3 1.0 copy.31
  558.4 18.1 %fusion = (f32[16,256]{1,0:T(8,128)S(1)}, f32[16,256,2048]{2,1,0:T(8,128)}) fusion(pred[256,2048]{1,0:T(8,128)(4,1)S(1)} %copy.31, bf16[2048,16,128]{0,2,1:T(8,128)(2,1)} %bitcast.243, bf16[256,2048]{1,0:T(8,128)(2,1)S(1)} %copy-done), kind=kOutput, calls=%fused_computation.4 | convolution fusion | flops 2172645376 | bytes 43532288 | tf_op jit(solution)/shard_map/thd,shd->hts/dot_general | solution.py:152
  576.4 16.5 %fusion.1 = f32[16,256]{1,0:T(8,128)S(1)} fusion(f32[16,256,2048]{2,1,0:T(8,128)} %get-tuple-element.45, f32[16,256]{1,0:T(8,128)S(1)} %broadcast_maximum_fusion, pred[256,2048]{1,0:T(8,128)(4,1)S(1)} %copy.31), kind=kLoop, calls=%fused_computation.5 | loop fusion | flops 41938944 | bytes 34111488 | tf_op jit(solution)/shard_map/reduce_sum | solution.py:158
  592.9 1.4 copy.35
  594.4 18.3 %all-gather.8.cloned.1.call-done = bf16[2048,2048]{0,1:T(8,128)(2,1)} async-done(((bf16[256,2048]{0,1:T(8,128)(2,1)}), bf16[2048,2048]{0,1:T(8,128)(2,1)}) %all-gather.8.cloned.1.call-update) | async-done | bytes 8388624 | tf_op jit(solution)/shard_map/all_gather | solution.py:140
  612.7 17.2 %fusion.52 = bf16[256,16,128]{0,2,1:T(8,128)(2,1)S(1)} fusion(bf16[2048,16,128]{0,2,1:T(8,128)(2,1)} %bitcast.249, f32[16,256,2048]{2,1,0:T(8,128)} %get-tuple-element.45, f32[16,256]{1,0:T(8,128)S(1)} %broadcast_maximum_fusion, pred[256,2048]{1,0:T(8,128)(4,1)S(1)} %copy.31, f32[256,16]{0,1:T(8,128)S(1)} %bitcast.248), kind=kOutput, calls=%fused_computation.122 | convolution fusion | flops 2190475264 | bytes 43548672 | tf_op jit(solution)/shard_map/hts,shd->htd/dot_general | solution.py:159
  629.9 1.4 copy.36
  (57 shorter events, 0.7 us)
Async XLA Ops:
  7.2 551.2 %copy-start = (bf16[256,2048]{1,0:T(8,128)(2,1)S(1)}, bf16[256,2048]{1,0:T(8,128)(2,1)}, u32[]{:S(2)}) copy-start(bf16[256,2048]{1,0:T(8,128)(2,1)} %param.17) | copy-start | bytes 3145732
  7.2 150.8 %all-gather.4.cloned.1.call-start = ((), (), s32[]{:S(2)}) async-start(), calls=%async_computation | async-start | bytes 2359296 | tf_op jit(solution)/shard_map/all_gather | solution.py:176
  14.1 26.3 %copy-start.5 = (bf16[256,2048]{0,1:T(8,128)(2,1)}, bf16[256,2048]{0,1:T(8,128)(2,1)S(1)}, u32[]{:S(2)}) copy-start(bf16[256,2048]{0,1:T(8,128)(2,1)S(1)} %get-tuple-element.26) | copy-start | bytes 3145732
  14.1 26.1 %collective-permute-start = (bf16[256,2048]{0,1:T(8,128)(2,1)S(1)}, bf16[256,2048]{0,1:T(8,128)(2,1)S(1)}, u32[]{:S(2)}, u32[]{:S(2)}) collective-permute-start(bf16[256,2048]{0,1:T(8,128)(2,1)S(1)} %get-tuple-element.26), channel_id=1, source_target_pairs={{0,16},{4,20},{8,24},{12,28},{16,0},{20,4},{24,8},{28,12},{1,17},{... | collective-permute-start | bytes 3145736 | tf_op jit(solution)/shard_map/ppermute | solution.py:18
  17.5 23.2 %copy-start.8 = (f32[1,256,2048]{1,2,0:T(8,128)S(1)}, f32[1,256,2048]{1,2,0:T(8,128)}, u32[]{:S(2)}) copy-start(f32[1,256,2048]{1,2,0:T(8,128)} %get-tuple-element.25) | copy-start | bytes 6291460
  44.9 4.1 copy-start.11
  47.2 100.5 %collective-permute-start.1 = (bf16[2,2,256,2048]{2,3,1,0:T(8,128)(2,1)}, bf16[2,2,256,2048]{2,3,1,0:T(8,128)(2,1)}, u32[]{:S(2)}, u32[]{:S(2)}) collective-permute-start(bf16[2,2,256,2048]{2,3,1,0:T(8,128)(2,1)} %pad_maximum_fusion.2), channel_id=1, source_target_pairs={{0,8},{4,12},{8,0},{12,4},{16,24},{20,28},{24,16},{28,20},{1,9},{5... | collective-permute-start | bytes 12582920 | tf_op jit(solution)/shard_map/ppermute | solution.py:18
  63.9 494.5 %all-gather.6.cloned.1.call-start = ((), (), s32[]{:S(2)}) async-start(), calls=%async_computation.1 | async-start | bytes 9437184 | tf_op jit(solution)/shard_map/all_gather | solution.py:139
  155.5 2.4 copy-start.12
  157.8 95.8 %collective-permute-start.2 = (bf16[2,2,256,2048]{2,3,1,0:T(8,128)(2,1)}, bf16[2,2,256,2048]{2,3,1,0:T(8,128)(2,1)}, u32[]{:S(2)}, u32[]{:S(2)}) collective-permute-start(bf16[2,2,256,2048]{2,3,1,0:T(8,128)(2,1)} %pad_maximum_fusion.3), channel_id=1, source_target_pairs={{0,4},{4,0},{8,12},{12,8},{16,20},{20,16},{24,28},{28,24},{1,5},{5... | collective-permute-start | bytes 12582920 | tf_op jit(solution)/shard_map/ppermute | solution.py:18
  270.7 4.7 copy-start.4
  298.4 7.0 %copy-start.1 = (f32[2,2048,256]{2,1,0:T(8,128)}, f32[2,2048,256]{2,1,0:T(8,128)S(1)}, u32[]{:S(2)}) copy-start(f32[2,2048,256]{2,1,0:T(8,128)S(1)} %convolution_subtract_fusion) | copy-start | bytes 12582916
  303.1 2.0 copy-start.2
  305.6 2.9 copy-start.9
  308.0 7.6 %collective-permute-start.3 = (bf16[2,2,256,2048]{2,3,1,0:T(8,128)(2,1)}, bf16[2,2,256,2048]{2,3,1,0:T(8,128)(2,1)}, u32[]{:S(2)}, u32[]{:S(2)}) collective-permute-start(bf16[2,2,256,2048]{2,3,1,0:T(8,128)(2,1)} %pad_maximum_fusion.4), channel_id=1, source_target_pairs={{0,4},{4,0},{8,12},{12,8},{16,20},{20,16},{24,28},{28,24},{1,5},{5... | collective-permute-start | bytes 12582920 | tf_op jit(solution)/shard_map/ppermute | solution.py:18
  309.8 302.9 %all-gather.8.cloned.1.call-start = ((), (), s32[]{:S(2)}) async-start(), calls=%async_computation.2 | async-start | bytes 9437184 | tf_op jit(solution)/shard_map/all_gather | solution.py:140
  326.8 118.5 %collective-permute-start.4 = (bf16[2,2,256,2048]{2,3,1,0:T(8,128)(2,1)}, bf16[2,2,256,2048]{2,3,1,0:T(8,128)(2,1)}, u32[]{:S(2)}, u32[]{:S(2)}) collective-permute-start(bf16[2,2,256,2048]{2,3,1,0:T(8,128)(2,1)} %pad_maximum_fusion.5), channel_id=1, source_target_pairs={{0,8},{4,12},{8,0},{12,4},{16,24},{20,28},{24,16},{28,20},{1,9},{5... | collective-permute-start | bytes 12582920 | tf_op jit(solution)/shard_map/ppermute | solution.py:18
  453.2 3.9 copy-start.10
  455.6 92.7 %collective-permute-start.5 = (bf16[2,2,256,2048]{2,3,1,0:T(8,128)(2,1)}, bf16[2,2,256,2048]{2,3,1,0:T(8,128)(2,1)}, u32[]{:S(2)}, u32[]{:S(2)}) collective-permute-start(bf16[2,2,256,2048]{2,3,1,0:T(8,128)(2,1)} %pad_maximum_fusion.6), channel_id=1, source_target_pairs={{0,16},{4,20},{8,24},{12,28},{16,0},{20,4},{24,8},{28,12},{1,17},{... | collective-permute-start | bytes 12582920 | tf_op jit(solution)/shard_map/ppermute | solution.py:18
  457.6 92.6 %copy-start.3 = (f32[2,256,2048]{1,2,0:T(8,128)S(1)}, f32[2,256,2048]{1,2,0:T(8,128)}, u32[]{:S(2)}) copy-start(f32[2,256,2048]{1,2,0:T(8,128)} %get-tuple-element.30) | copy-start | bytes 12582916
  550.2 4.3 copy-start.6
  550.2 4.3 copy-start.13
  554.5 2.1 copy-start.14
  576.4 16.5 %copy-start.7 = (bf16[256,2048]{0,1:T(8,128)(2,1)S(1)}, bf16[256,2048]{0,1:T(8,128)(2,1)}, u32[]{:S(2)}) copy-start(bf16[256,2048]{0,1:T(8,128)(2,1)} %fusion.39) | copy-start | bytes 3145732
Sparse Core Ops, SparseCore 0:
  64.0 36.5 all-gather.3
  309.9 80.3 all-gather.5
  556.7 55.9 all-gather.7
where the time goes:
time: 643 us; the launch traced here: 638 us
  waiting for transfers between devices  338 us (53%)
  matrix products  128 us (20%)
  other arithmetic  81.2 us (13%)
  local copies, waits for them, and re-layouts  53.4 us (8%)
  blocking collectives  14.9 us (2%)
  between operations  14.5 us (2%)
  starting transfers between devices  8.37 us (1%)
    ppermute x6, waiting for transfers between devices, swapped(): return lax.ppermute(value, axis, pairs)  320 us
    dot_general x8, matrix products, apply_matrix(): return jnp.einsum('km,emc->ekc', matrix, data, precision=highest)  43.9 us
    another operation x11, other arithmetic, butterfly_conv(): received = swapped(shortened(jnp.stack(state)), 'seq', level)  40.9 us
    dot_general x1, matrix products, butterfly_conv(): table_im = -jnp.dot(bank, jnp.sin(angles), precision=highest)  24.5 us
    dot_general x1, matrix products, butterfly_conv(): table_re = jnp.dot(bank, jnp.cos(angles), precision=highest)  23.5 us
    all_gather x1, waiting for transfers between devices, attention(): value_piece = lax.all_gather(hyena_out, 'seq', axis=0, tiled=True)  18.3 us
    dot_general x1, matrix products, attention(): jnp.einsum('thd,shd->hts', queries, keys_here, preferred_element_type=jnp...  18.1 us
    dot_general x1, matrix products, attention(): jnp.einsum('hts,shd->htd', weights.astype(jnp.bfloat16), values_here, pre...  17.2 us
  transfers between devices with their start and end apart: 9, of which 6 were waited for; matrix products, arithmetic and copies ran while one was open for 28% of the time, Pallas kernels for 0%

commit v1 on v0

--- a/solution.py
+++ b/solution.py
@@ -1,8 +1,13 @@
+import functools
 import math
 
 import jax
 import jax.numpy as jnp
+import ml_dtypes
+import numpy as np
 from jax import lax
+from jax.experimental import pallas as pl
+from jax.experimental.pallas import tpu as pltpu
 from jax.sharding import PartitionSpec as P
 
 HD = 128
@@ -182,9 +187,354 @@
     return (hyena_out, attn_out)
 
 
+MIXED, SELECT, GATE, QUERY, KEY, HYENA, ATTN, MASK = range(8)
+
+
+def half_step_dft(block):
+    freqs = np.concatenate([np.arange(0, block, 2), np.arange(1, block, 2)])
+    steps = (2 * freqs[:, None] + 1) * np.arange(block)[None, :] % (4 * block)
+    angles = steps * (math.pi / (2 * block))
+    forward = np.concatenate([np.cos(angles), -np.sin(angles)], axis=0)
+    inverse = forward.T / block
+    return forward.astype(ml_dtypes.bfloat16), inverse.astype(ml_dtypes.bfloat16)
+
+
+def fused_kernel(
+    n, m,
+    hk, hv, fil, grp, bias, mask, fwd, inv, hq, aq, ak,
+    hy, at,
+    mixed, select, bank, masks, mixed_in, select_in, gate_in, query_in, key_in,
+    values, result, mask_add, spec, fspec,
+    bank_send, bank_recv, send, recv, local,
+):
+    me = lax.axis_index("seq")
+    plane = lax.axis_index("chan")
+    rows = hk.shape[0]
+    wide = hk.shape[1] // n
+    subs = rows // ABLK
+    heads = wide // HD
+    bf16, f32 = jnp.bfloat16, jnp.float32
+
+    barrier = pltpu.get_barrier_semaphore()
+    for d in range(1, n):
+        pl.semaphore_signal(
+            barrier, inc=1, device_id={"seq": lax.rem(me + d, n)},
+            device_id_type=pl.DeviceIdType.MESH,
+        )
+    for d in range(1, m):
+        pl.semaphore_signal(
+            barrier, inc=1, device_id={"chan": lax.rem(plane + d, m)},
+            device_id_type=pl.DeviceIdType.MESH,
+        )
+
+    def columns(p):
+        return pl.ds(pl.multiple_of(p * wide, wide), wide)
+
+    def seq_copy(kind, d, src, dst):
+        return pltpu.make_async_remote_copy(
+            src_ref=src, dst_ref=dst, send_sem=send.at[kind, d], recv_sem=recv.at[kind, d],
+            device_id={"seq": lax.rem(me + d, n)}, device_id_type=pl.DeviceIdType.MESH,
+        )
+
+    def bank_copy(d):
+        return pltpu.make_async_remote_copy(
+            src_ref=bank.at[plane], dst_ref=bank.at[plane],
+            send_sem=bank_send.at[d], recv_sem=bank_recv.at[d],
+            device_id={"chan": lax.rem(plane + d, m)}, device_id_type=pl.DeviceIdType.MESH,
+        )
+
+    def mixed_copy(d):
+        return seq_copy(MIXED, d, mixed.at[lax.rem(me + d, n)], mixed_in.at[me])
+
+    def select_copy(d):
+        return seq_copy(SELECT, d, select.at[lax.rem(me + d, n)], select_in.at[me])
+
+    def gate_copy(d):
+        return seq_copy(GATE, d, hq.at[:, columns(lax.rem(me + d, n))], gate_in.at[me])
+
+    def query_copy(d):
+        return seq_copy(QUERY, d, aq.at[:, columns(lax.rem(me + d, n))], query_in.at[me])
+
+    def key_copy(d):
+        return seq_copy(KEY, d, ak.at[:, columns(lax.rem(me + d, n))], key_in.at[me])
+
+    def hyena_copy(d):
+        return seq_copy(HYENA, d, values.at[lax.rem(me + d, n)], hy.at[:, columns(me)])
+
+    def attn_copy(d):
+        return seq_copy(ATTN, d, result.at[lax.rem(me + d, n)], at.at[:, columns(me)])
+
+    def mask_copy(d):
+        return seq_copy(MASK, d, masks.at[me], masks.at[me])
+
+    own_in = [
+        pltpu.make_async_copy(src.at[:, columns(me)], dst.at[me], local.at[i])
+        for i, (src, dst) in enumerate([(hq, gate_in), (aq, query_in), (ak, key_in)])
+    ]
+    for copy in own_in:
+        copy.start()
+
+    bank[plane] = fil[...].T.astype(bf16)
+    masks[me] = jnp.zeros(masks.shape[1:], f32)
+    masks[me, 0:subs, 0:mask.shape[1]] = mask[...].astype(f32)
+    for p in range(n):
+        part = slice(p * wide, (p + 1) * wide)
+        mixed[p] = (hk[:, part].astype(f32) * hv[:, part].astype(f32)).astype(bf16)
+
+    pl.semaphore_wait(barrier, n + m - 2)
+    for d in range(1, m):
+        bank_copy(d).start()
+    for d in range(1, n):
+        mixed_copy(d).start()
+    for d in range(1, n):
+        mask_copy(d).start()
+
+    mixed_in[me] = mixed[me]
+
+    for d in range(1, m):
+        bank_copy(d).wait()
+
+    def chosen(p):
+        table = jnp.concatenate([bank[k] for k in range(m)], axis=1)
+        index = lax.broadcasted_iota(jnp.int32, (table.shape[1], wide), 0)
+        onehot = jnp.where(index == grp[p], 1.0, 0.0).astype(bf16)
+        return jnp.dot(table, onehot, preferred_element_type=f32).astype(bf16)
+
+    def choose(d, carry):
+        p = lax.rem(me + d, n)
+        select[p] = chosen(p)
+        select_copy(d).start()
+        return carry
+
+    lax.fori_loop(1, n, choose, 0)
+    select_in[me] = chosen(me)
+
+    spec[me] = jnp.dot(fwd[...], mixed_in[me], preferred_element_type=f32)
+    fspec[me] = jnp.dot(fwd[...], select_in[me], preferred_element_type=f32)
+
+    def signal_step(d, carry):
+        mixed_copy(d).wait()
+        i = lax.rem(me + n - d, n)
+        spec[i] = jnp.dot(fwd[...], mixed_in[i], preferred_element_type=f32)
+        return carry
+
+    lax.fori_loop(1, n, signal_step, 0)
+    for d in range(1, n):
+        gate_copy(d).start()
+
+    def filter_step(d, carry):
+        select_copy(d).wait()
+        i = lax.rem(me + n - d, n)
+        fspec[i] = jnp.dot(fwd[...], select_in[i], preferred_element_type=f32)
+        return carry
+
+    lax.fori_loop(1, n, filter_step, 0)
+    for d in range(1, n):
+        query_copy(d).start()
+    for d in range(1, n):
+        key_copy(d).start()
+
+    tiles = rows // 8
+
+    def product(t, carry):
+        re = pl.ds(pl.multiple_of(t * 8, 8), 8)
+        im = pl.ds(pl.multiple_of(rows + t * 8, 8), 8)
+        turn = jnp.where(t < tiles // 2, 1.0, -1.0).astype(f32)
+        for lane in range(0, wide, 128):
+            lanes = slice(lane, lane + 128)
+            xr = [spec[i, re, lanes] for i in range(n)]
+            xi = [spec[i, im, lanes] for i in range(n)]
+            gr = [fspec[i, re, lanes] for i in range(n)]
+            gi = [fspec[i, im, lanes] for i in range(n)]
+            last_re = last_im = None
+            for j in range(n):
+                sum_re = sum_im = None
+                for i in range(j + 1):
+                    a, b, c, e = xr[i], xi[i], gr[j - i], gi[j - i]
+                    new_re, new_im = a * c - b * e, a * e + b * c
+                    sum_re = new_re if sum_re is None else sum_re + new_re
+                    sum_im = new_im if sum_im is None else sum_im + new_im
+                if j == 0:
+                    spec[j, re, lanes] = sum_re
+                    spec[j, im, lanes] = sum_im
+                else:
+                    spec[j, re, lanes] = sum_re - turn * last_im
+                    spec[j, im, lanes] = sum_im + turn * last_re
+                last_re, last_im = sum_re, sum_im
+        return carry
+
+    lax.fori_loop(0, tiles, product, 0)
+
+    own_in[0].wait()
+
+    def finish(j):
+        conv = jnp.dot(inv[...], spec[j].astype(bf16), preferred_element_type=f32)
+        direct = bias[me] * mixed_in[j].astype(f32)
+        values[j] = (gate_in[j].astype(f32) * (conv + direct)).astype(bf16)
+
+    def hyena_step(d, carry):
+        gate_copy(n - d).wait()
+        finish(lax.rem(me + d, n))
+        hyena_copy(d).start()
+        return carry
+
+    lax.fori_loop(1, n, hyena_step, 0)
+    finish(me)
+    own_hyena = pltpu.make_async_copy(values.at[me], hy.at[:, columns(me)], local.at[3])
+    own_hyena.start()
+
+    for d in range(1, n):
+        mask_copy(d).wait()
+    flags = masks[...].reshape(n * masks.shape[1], masks.shape[2]).astype(bf16)
+    for k in range(n):
+        block_id = lax.broadcasted_iota(jnp.int32, (masks.shape[2], rows), 0)
+        owner = lax.broadcasted_iota(jnp.int32, (masks.shape[2], rows), 1) // ABLK + k * subs
+        spread = jnp.where(block_id == owner, 1.0, 0.0).astype(bf16)
+        shown = jnp.dot(flags, spread, preferred_element_type=f32)
+        mask_add[:, k] = ((shown - 1.0) * 1e30).reshape(n, masks.shape[1], rows)
+
+    own_in[1].wait()
+    own_in[2].wait()
+    for d in range(1, n):
+        query_copy(d).wait()
+    for d in range(1, n):
+        key_copy(d).wait()
+    scale = HD ** (-0.5)
+
+    def attend(r):
+
+        def scores(h, k, add):
+            part = slice(h * HD, (h + 1) * HD)
+            raw = lax.dot_general(
+                query_in[r, :, part], key_in[k, :, part], (((1,), (1,)), ((), ())),
+                preferred_element_type=f32,
+            )
+            return raw + add
+
+        def weighted(h, k, weights):
+            part = slice(h * HD, (h + 1) * HD)
+            return jnp.dot(weights.astype(bf16), values[k, :, part], preferred_element_type=f32)
+
+        def added(k):
+            flags_here = mask_add[r, k]
+            return jnp.concatenate(
+                [jnp.broadcast_to(flags_here[i : i + 1], (ABLK, rows)) for i in range(subs)], axis=0
+            )
+
+        row = lax.broadcasted_iota(jnp.int32, (rows, rows), 0)
+        col = lax.broadcasted_iota(jnp.int32, (rows, rows), 1)
+        add = jnp.where(col <= row, added(r), -1e30)
+        state = []
+        for h in range(heads):
+            here = scores(h, r, add)
+            top = jnp.max(here, axis=1, keepdims=True)
+            weights = jnp.exp((here - top) * scale)
+            state.append((top, jnp.sum(weights, axis=1, keepdims=True), weighted(h, r, weights)))
+
+        def step(k, state):
+            add = added(k)
+            out = []
+            for h in range(heads):
+                top, total, acc = state[h]
+                here = scores(h, k, add)
+                new_top = jnp.maximum(top, jnp.max(here, axis=1, keepdims=True))
+                weights = jnp.exp((here - new_top) * scale)
+                keep = jnp.exp((top - new_top) * scale)
+                total = total * keep + jnp.sum(weights, axis=1, keepdims=True)
+                out.append((new_top, total, acc * keep + weighted(h, k, weights)))
+            return tuple(out)
+
+        state = lax.fori_loop(0, r, step, tuple(state))
+        for h in range(heads):
+            result[r, :, h * HD : (h + 1) * HD] = (state[h][2] / state[h][1]).astype(bf16)
+
+    def attn_step(d, carry):
+        attend(lax.rem(me + d, n))
+        attn_copy(d).start()
+        return carry
+
+    lax.fori_loop(1, n, attn_step, 0)
+    attend(me)
+    own_attn = pltpu.make_async_copy(result.at[me], at.at[:, columns(me)], local.at[4])
+    own_attn.start()
+    own_hyena.wait()
+    own_attn.wait()
+    for d in range(1, n):
+        hyena_copy(d).wait()
+    for d in range(1, n):
+        attn_copy(d).wait()
+
+
+def fused_on_device(
+    n, m, hyena_query, hyena_key, hyena_value, bias, groups, filters, att_queries, att_keys, block_mask
+):
+    rows, channels = hyena_key.shape
+    wide = channels // n
+    lanes = filters.shape[0]
+    forward, inverse = half_step_dft(rows)
+    bf16, f32 = jnp.bfloat16, jnp.float32
+    blocks = pltpu.VMEM((n, rows, wide), bf16)
+    vmem = pl.BlockSpec(memory_space=pltpu.VMEM)
+    anywhere = pl.BlockSpec(memory_space=pl.ANY)
+    return pl.pallas_call(
+        functools.partial(fused_kernel, n, m),
+        out_shape=[jax.ShapeDtypeStruct((rows, channels), bf16)] * 2,
+        in_specs=[vmem] * 8 + [anywhere] * 3,
+        out_specs=[anywhere] * 2,
+        scratch_shapes=[
+            blocks,
+            blocks,
+            pltpu.VMEM((m, rows, lanes), bf16),
+            pltpu.VMEM((n, 8, 128), f32),
+            blocks,
+            blocks,
+            blocks,
+            blocks,
+            blocks,
+            blocks,
+            blocks,
+            pltpu.VMEM((n, n, 8, rows), f32),
+            pltpu.VMEM((n, 2 * rows, wide), f32),
+            pltpu.VMEM((n, 2 * rows, wide), f32),
+            pltpu.SemaphoreType.DMA((m,)),
+            pltpu.SemaphoreType.DMA((m,)),
+            pltpu.SemaphoreType.DMA((8, n)),
+            pltpu.SemaphoreType.DMA((8, n)),
+            pltpu.SemaphoreType.DMA((5,)),
+        ],
+        compiler_params=pltpu.CompilerParams(
+            collective_id=0, has_side_effects=True, vmem_limit_bytes=52 * 1024 * 1024
+        ),
+        name="hyena_attention",
+    )(
+        hyena_key, hyena_value, filters,
+        groups.reshape(n, 1, wide), bias.reshape(n, 1, wide), block_mask,
+        jnp.asarray(forward), jnp.asarray(inverse),
+        hyena_query, att_queries, att_keys,
+    )
+
+
+def by_shape(
+    n, m, hyena_query, hyena_key, hyena_value, bias, groups, filters, att_queries, att_keys, block_mask
+):
+    rows, channels = hyena_key.shape
+    fits = (
+        channels % (n * HD) == 0
+        and rows % (2 * ABLK) == 0
+        and rows // ABLK <= 8
+        and block_mask.shape[1] <= 128
+        and filters.shape[0] % 128 == 0
+        and filters.shape[1] == rows
+    )
+    args = (
+        hyena_query, hyena_key, hyena_value, bias, groups, filters, att_queries, att_keys, block_mask
+    )
+    return fused_on_device(n, m, *args) if fits else on_device(*args)
+
+
 def solution(mesh):
     return jax.shard_map(
-        on_device,
+        functools.partial(by_shape, mesh.shape["seq"], mesh.shape["chan"]),
         mesh=mesh,
         in_specs=(
             P("seq", "chan"),

time: 643 us -> 105 us (0.16)
  waiting for transfers between devices: 338 us -> 0 us
  matrix products: 128 us -> 0 us
  Pallas kernels: 0 us -> 96.3 us
  other arithmetic: 81.2 us -> 0 us
  local copies, waits for them, and re-layouts: 53.4 us -> 7.43 us
  blocking collectives: 14.9 us -> 0 us
  between operations: 14.5 us -> 0.66 us
  starting transfers between devices: 8.37 us -> 0 us
    ppermute x6 -> x0, waiting for transfers between devices: 320 us -> none  [swapped(): return lax.ppermute(value, axis, pairs)]
    dot_general x13 -> x0, matrix products: 128 us -> none  [the longest x8 43.9 us: apply_matrix(): return jnp.einsum('km,emc->ekc', matrix, data, precision=highest)]
    pallas_call x0 -> x1, Pallas kernels: none -> 96.3 us  [fused_on_device(): pl.pallas_call(functools.partial(fused_kernel, n, m), out_shape=[jax.Shap...]
    another operation x17 -> x0, other arithmetic: 44.6 us -> none  [the longest x11 40.9 us: butterfly_conv(): received = swapped(shortened(jnp.stack(state)), 'seq', level)]
    all_gather x3 -> x0, waiting for transfers between devices: 18.4 us -> none  [the longest x1 18.3 us: attention(): value_piece = lax.all_gather(hyena_out, 'seq', axis=0, tiled=True)]
    gather x2 -> x0, local copies, waits for them, and re-layouts: 18.3 us -> none  [the longest x1 9.35 us: butterfly_conv(): jnp.take(table_re, groups, axis=0).T.reshape(2, rows_dev, channels)]
    reduce_sum x1 -> x0, other arithmetic: 16.5 us -> none  [attention(): new_total = jnp.sum(weights, axis=-1)]
    all_gather x1 -> x0, blocking collectives: 14.9 us -> none  [on_device(): lax.all_gather(filters.astype(jnp.bfloat16), 'chan', axis=0, tiled=True)]
  transfers between devices with their start and end apart: 9 -> 0, of which waited for: 6 -> 0; matrix products, arithmetic and copies ran while one was open for 28% -> 0% of each run, Pallas kernels for 0% -> 0%
where the time goes in v1:
time: 105 us; the launch traced here: 104 us
  Pallas kernels  96.3 us (92%)
  local copies, waits for them, and re-layouts  7.43 us (7%)
    pallas_call x1, Pallas kernels, fused_on_device(): pl.pallas_call(functools.partial(fused_kernel, n, m), out_shape=[jax.Shap...  96.3 us
    unnamed x16, local copies, waits for them, and re-layouts  7.43 us

profile of v1, /device:TPU:0, one launch (start us, length us, event | category | flops | bytes accessed | tf_op | source)
XLA Modules:
  0.0 104.4 jit_solution(3947996196141938795)
XLA Ops:
  0.6 0.0 copy-start.5
  0.6 0.7 copy-done.5
  1.3 0.0 copy-start
  1.3 0.9 copy-done
  2.3 0.0 copy-start.1
  2.3 0.9 copy-done.1
  3.2 0.0 copy-start.2
  3.2 0.9 copy-done.2
  4.1 0.0 copy-start.3
  4.1 0.7 copy-done.3
  4.8 0.0 copy-start.4
  4.8 0.7 copy-done.4
  5.5 96.3 %hyena_attention.1 = (bf16[256,2048]{1,0:T(8,128)(2,1)S(1)}, bf16[256,2048]{1,0:T(8,128)(2,1)}) custom-call(bf16[256,2048]{1,0:T(8,128)(2,1)} %hk.1, bf16[256,2048]{1,0:T(8,128)(2,1)} %hv.1, f32[128,256]{1,0:T(8,128)S(1)} %copy-done.2, s32[8,1,256]{2,1,0:T(1,128)S(1)} %bitcast.2, f32[8,1,256]{2,1,0:T(1,128)S(1)} %bitcast.3, s32[2,16]{1,0:T(2,128)S(1)} %copy-done.5, ...), custom_call_target="tpu_custom_call" | custom-call | tf_op jit(solution)/shard_map/hyena_attention/pallas_call | solution.py:479
  101.8 0.0 copy-start.6
  101.8 1.0 copy.15
  102.8 0.6 copy-done.6
  103.4 1.0 copy.16
Async XLA Ops:
  0.6 0.7 copy-start.5
  1.3 0.9 copy-start
  2.3 0.9 copy-start.1
  3.2 0.9 copy-start.2
  4.1 0.7 copy-start.3
  4.8 0.7 copy-start.4
  101.8 1.6 %copy-start.6 = (bf16[256,2048]{1,0:T(8,128)(2,1)S(1)}, bf16[256,2048]{1,0:T(8,128)(2,1)}, u32[]{:S(2)}) copy-start(bf16[256,2048]{1,0:T(8,128)(2,1)} %get-tuple-element.5) | copy-start | bytes 3145732

commit v2 on v1

--- a/solution.py
+++ b/solution.py
@@ -187,7 +187,7 @@
     return (hyena_out, attn_out)
 
 
-MIXED, SELECT, GATE, QUERY, KEY, HYENA, ATTN, MASK = range(8)
+MIXED, GATE, QUERY, KEY, HYENA, ATTN, MASK = range(7)
 
 
 def half_step_dft(block):
@@ -201,14 +201,19 @@
 
 def fused_kernel(
     n, m,
-    hk, hv, fil, grp, bias, mask, fwd, inv, hq, aq, ak,
+    hk_far, hv_far, fil_far, grp_far, bias_far, mask_far, fwd_far, inv_far, hq, aq, ak,
     hy, at,
-    mixed, select, bank, masks, mixed_in, select_in, gate_in, query_in, key_in,
+    hk, hv, fil, grp, bias, mask, fwd, inv,
+    mixed, select, bank, hot, masks, mixed_in, select_in, gate_in, query_in, key_in,
     values, result, mask_add, spec, fspec,
-    bank_send, bank_recv, send, recv, local,
+    lag_send, lag_recv, bank_send, bank_recv, pair_send, pair_recv, send, recv, local, loads,
 ):
     me = lax.axis_index("seq")
     plane = lax.axis_index("chan")
+    side = lax.rem(me, 2)
+    sibling = me + 1 - 2 * side
+    pair = lax.div(me, 2)
+    pairs = n // 2
     rows = hk.shape[0]
     wide = hk.shape[1] // n
     subs = rows // ABLK
@@ -236,18 +241,31 @@
             device_id={"seq": lax.rem(me + d, n)}, device_id_type=pl.DeviceIdType.MESH,
         )
 
-    def bank_copy(d):
+    def lag_copy(e):
         return pltpu.make_async_remote_copy(
-            src_ref=bank.at[plane], dst_ref=bank.at[plane],
-            send_sem=bank_send.at[d], recv_sem=bank_recv.at[d],
+            src_ref=bank.at[plane, pair], dst_ref=bank.at[plane, pair],
+            send_sem=lag_send.at[e], recv_sem=lag_recv.at[e],
+            device_id={"seq": lax.rem(me + 2 * e, n)}, device_id_type=pl.DeviceIdType.MESH,
+        )
+
+    def bank_copy(e, d):
+        part = lax.rem(pair + pairs - e, pairs)
+        return pltpu.make_async_remote_copy(
+            src_ref=bank.at[plane, part], dst_ref=bank.at[plane, part],
+            send_sem=bank_send.at[e, d], recv_sem=bank_recv.at[e, d],
             device_id={"chan": lax.rem(plane + d, m)}, device_id_type=pl.DeviceIdType.MESH,
         )
 
+    def pair_copy(e):
+        part = 2 * lax.rem(pair + pairs - e, pairs) + side
+        return pltpu.make_async_remote_copy(
+            src_ref=select.at[e], dst_ref=select_in.at[part],
+            send_sem=pair_send.at[e], recv_sem=pair_recv.at[e],
+            device_id={"seq": sibling}, device_id_type=pl.DeviceIdType.MESH,
+        )
+
     def mixed_copy(d):
         return seq_copy(MIXED, d, mixed.at[lax.rem(me + d, n)], mixed_in.at[me])
-
-    def select_copy(d):
-        return seq_copy(SELECT, d, select.at[lax.rem(me + d, n)], select_in.at[me])
 
     def gate_copy(d):
         return seq_copy(GATE, d, hq.at[:, columns(lax.rem(me + d, n))], gate_in.at[me])
@@ -274,43 +292,51 @@
     for copy in own_in:
         copy.start()
 
-    bank[plane] = fil[...].T.astype(bf16)
+    near = [
+        pltpu.make_async_copy(src, dst, loads.at[i])
+        for i, (src, dst) in enumerate([
+            (fil_far, fil), (mask_far, mask), (hk_far, hk), (hv_far, hv),
+            (grp_far, grp), (fwd_far, fwd), (inv_far, inv), (bias_far, bias),
+        ])
+    ]
+    for copy in near:
+        copy.start()
+
+    near[0].wait()
+    near[1].wait()
+    bank[plane, pair] = fil[...].T.astype(bf16)
     masks[me] = jnp.zeros(masks.shape[1:], f32)
-    masks[me, 0:subs, 0:mask.shape[1]] = mask[...].astype(f32)
+    masks[me, 0:subs, 0 : mask.shape[1]] = mask[...].astype(f32)
+    near[2].wait()
+    near[3].wait()
     for p in range(n):
         part = slice(p * wide, (p + 1) * wide)
         mixed[p] = (hk[:, part].astype(f32) * hv[:, part].astype(f32)).astype(bf16)
 
     pl.semaphore_wait(barrier, n + m - 2)
+    for e in range(1, pairs):
+        lag_copy(e).start()
     for d in range(1, m):
-        bank_copy(d).start()
+        bank_copy(0, d).start()
     for d in range(1, n):
         mixed_copy(d).start()
     for d in range(1, n):
         mask_copy(d).start()
 
     mixed_in[me] = mixed[me]
-
-    for d in range(1, m):
-        bank_copy(d).wait()
-
-    def chosen(p):
-        table = jnp.concatenate([bank[k] for k in range(m)], axis=1)
-        index = lax.broadcasted_iota(jnp.int32, (table.shape[1], wide), 0)
-        onehot = jnp.where(index == grp[p], 1.0, 0.0).astype(bf16)
-        return jnp.dot(table, onehot, preferred_element_type=f32).astype(bf16)
-
-    def choose(d, carry):
-        p = lax.rem(me + d, n)
-        select[p] = chosen(p)
-        select_copy(d).start()
-        return carry
-
-    lax.fori_loop(1, n, choose, 0)
-    select_in[me] = chosen(me)
-
+    near[4].wait()
+    lanes_here = bank.shape[3]
+    for which, owner in enumerate((me, sibling)):
+        index = lax.broadcasted_iota(jnp.int32, (m * lanes_here, wide), 0)
+        hot[which] = jnp.where(index == grp[owner], 1.0, 0.0).astype(bf16)
+
+    for e in range(1, pairs):
+        lag_copy(e).wait()
+        for d in range(1, m):
+            bank_copy(e, d).start()
+
+    near[5].wait()
     spec[me] = jnp.dot(fwd[...], mixed_in[me], preferred_element_type=f32)
-    fspec[me] = jnp.dot(fwd[...], select_in[me], preferred_element_type=f32)
 
     def signal_step(d, carry):
         mixed_copy(d).wait()
@@ -318,21 +344,33 @@
         spec[i] = jnp.dot(fwd[...], mixed_in[i], preferred_element_type=f32)
         return carry
 
-    lax.fori_loop(1, n, signal_step, 0)
+    lax.fori_loop(1, n // 2 + 1, signal_step, 0)
     for d in range(1, n):
         gate_copy(d).start()
-
-    def filter_step(d, carry):
-        select_copy(d).wait()
-        i = lax.rem(me + n - d, n)
-        fspec[i] = jnp.dot(fwd[...], select_in[i], preferred_element_type=f32)
-        return carry
-
-    lax.fori_loop(1, n, filter_step, 0)
-    for d in range(1, n):
-        query_copy(d).start()
-    for d in range(1, n):
-        key_copy(d).start()
+    lax.fori_loop(n // 2 + 1, n, signal_step, 0)
+
+    def chosen(part, which):
+        table = jnp.concatenate([bank[k, part] for k in range(m)], axis=1)
+        return jnp.dot(table, hot[which], preferred_element_type=f32).astype(bf16)
+
+    for e in range(pairs):
+        for d in range(1, m):
+            bank_copy(e, d).wait()
+        part = lax.rem(pair + pairs - e, pairs)
+        select[e] = chosen(part, 1)
+        pair_copy(e).start()
+        own = 2 * part + side
+        fspec[own] = jnp.dot(fwd[...], chosen(part, 0), preferred_element_type=f32)
+        if e == 0:
+            for d in range(1, n):
+                query_copy(d).start()
+        if e == min(1, pairs - 1):
+            for d in range(1, n):
+                key_copy(d).start()
+    for e in range(pairs):
+        pair_copy(e).wait()
+        other = 2 * lax.rem(pair + pairs - e, pairs) + 1 - side
+        fspec[other] = jnp.dot(fwd[...], select_in[other], preferred_element_type=f32)
 
     tiles = rows // 8
 
@@ -366,6 +404,8 @@
     lax.fori_loop(0, tiles, product, 0)
 
     own_in[0].wait()
+    near[6].wait()
+    near[7].wait()
 
     def finish(j):
         conv = jnp.dot(inv[...], spec[j].astype(bf16), preferred_element_type=f32)
@@ -375,7 +415,6 @@
     def hyena_step(d, carry):
         gate_copy(n - d).wait()
         finish(lax.rem(me + d, n))
-        hyena_copy(d).start()
         return carry
 
     lax.fori_loop(1, n, hyena_step, 0)
@@ -397,9 +436,19 @@
     own_in[2].wait()
     for d in range(1, n):
         query_copy(d).wait()
-    for d in range(1, n):
+    for d in range(1, n // 2 + 1):
         key_copy(d).wait()
-    scale = HD ** (-0.5)
+    for d in range(1, n):
+        hyena_copy(d).start()
+    for d in range(n // 2 + 1, n):
+        key_copy(d).wait()
+    scale = HD ** (-0.5) / math.log(2.0)
+
+    def lane_sum(weights):
+        total = weights[:, 0:128]
+        for lane in range(128, rows, 128):
+            total = total + weights[:, lane : lane + 128]
+        return total
 
     def attend(r):
 
@@ -428,8 +477,8 @@
         for h in range(heads):
             here = scores(h, r, add)
             top = jnp.max(here, axis=1, keepdims=True)
-            weights = jnp.exp((here - top) * scale)
-            state.append((top, jnp.sum(weights, axis=1, keepdims=True), weighted(h, r, weights)))
+            weights = jnp.exp2((here - top) * scale)
+            state.append((top, lane_sum(weights), weighted(h, r, weights)))
 
         def step(k, state):
             add = added(k)
@@ -438,15 +487,16 @@
                 top, total, acc = state[h]
                 here = scores(h, k, add)
                 new_top = jnp.maximum(top, jnp.max(here, axis=1, keepdims=True))
-                weights = jnp.exp((here - new_top) * scale)
-                keep = jnp.exp((top - new_top) * scale)
-                total = total * keep + jnp.sum(weights, axis=1, keepdims=True)
+                weights = jnp.exp2((here - new_top) * scale)
+                keep = jnp.exp2((top - new_top) * scale)
+                total = total * keep + lane_sum(weights)
                 out.append((new_top, total, acc * keep + weighted(h, k, weights)))
             return tuple(out)
 
         state = lax.fori_loop(0, r, step, tuple(state))
         for h in range(heads):
-            result[r, :, h * HD : (h + 1) * HD] = (state[h][2] / state[h][1]).astype(bf16)
+            total = jnp.sum(state[h][1], axis=1, keepdims=True)
+            result[r, :, h * HD : (h + 1) * HD] = (state[h][2] / total).astype(bf16)
 
     def attn_step(d, carry):
         attend(lax.rem(me + d, n))
@@ -465,26 +515,50 @@
         attn_copy(d).wait()
 
 
+def copy_kernel(parts, hy, at, hy_out, at_out, sems):
+    step = hy.shape[0] // parts
+    copies = []
+    for i, (src, dst) in enumerate([(hy, hy_out), (at, at_out)]):
+        for k in range(parts):
+            part = pl.ds(k * step, step)
+            copies.append(pltpu.make_async_copy(src.at[part], dst.at[part], sems.at[i, k]))
+    for copy in copies:
+        copy.start()
+    for copy in copies:
+        copy.wait()
+
+
 def fused_on_device(
     n, m, hyena_query, hyena_key, hyena_value, bias, groups, filters, att_queries, att_keys, block_mask
 ):
     rows, channels = hyena_key.shape
     wide = channels // n
     lanes = filters.shape[0]
+    pairs = n // 2
     forward, inverse = half_step_dft(rows)
     bf16, f32 = jnp.bfloat16, jnp.float32
     blocks = pltpu.VMEM((n, rows, wide), bf16)
-    vmem = pl.BlockSpec(memory_space=pltpu.VMEM)
     anywhere = pl.BlockSpec(memory_space=pl.ANY)
-    return pl.pallas_call(
+    dma = pltpu.SemaphoreType.DMA
+    outs = [jax.ShapeDtypeStruct((rows, channels), bf16)] * 2
+    hyena_out, attn_out = pl.pallas_call(
         functools.partial(fused_kernel, n, m),
-        out_shape=[jax.ShapeDtypeStruct((rows, channels), bf16)] * 2,
-        in_specs=[vmem] * 8 + [anywhere] * 3,
+        out_shape=outs,
+        in_specs=[anywhere] * 11,
         out_specs=[anywhere] * 2,
         scratch_shapes=[
-            blocks,
-            blocks,
-            pltpu.VMEM((m, rows, lanes), bf16),
+            pltpu.VMEM((rows, channels), bf16),
+            pltpu.VMEM((rows, channels), bf16),
+            pltpu.VMEM(filters.shape, f32),
+            pltpu.VMEM((n, 1, wide), jnp.int32),
+            pltpu.VMEM((n, 1, wide), f32),
+            pltpu.VMEM(block_mask.shape, jnp.int32),
+            pltpu.VMEM(forward.shape, bf16),
+            pltpu.VMEM(inverse.shape, bf16),
+            blocks,
+            pltpu.VMEM((pairs, rows, wide), bf16),
+            pltpu.VMEM((m, pairs, rows, lanes), bf16),
+            pltpu.VMEM((2, m * lanes, wide), bf16),
             pltpu.VMEM((n, 8, 128), f32),
             blocks,
             blocks,
@@ -496,14 +570,19 @@
             pltpu.VMEM((n, n, 8, rows), f32),
             pltpu.VMEM((n, 2 * rows, wide), f32),
             pltpu.VMEM((n, 2 * rows, wide), f32),
-            pltpu.SemaphoreType.DMA((m,)),
-            pltpu.SemaphoreType.DMA((m,)),
-            pltpu.SemaphoreType.DMA((8, n)),
-            pltpu.SemaphoreType.DMA((8, n)),
-            pltpu.SemaphoreType.DMA((5,)),
+            dma((pairs,)),
+            dma((pairs,)),
+            dma((pairs, m)),
+            dma((pairs, m)),
+            dma((pairs,)),
+            dma((pairs,)),
+            dma((7, n)),
+            dma((7, n)),
+            dma((5,)),
+            dma((8,)),
         ],
         compiler_params=pltpu.CompilerParams(
-            collective_id=0, has_side_effects=True, vmem_limit_bytes=52 * 1024 * 1024
+            collective_id=0, has_side_effects=True, vmem_limit_bytes=60 * 1024 * 1024
         ),
         name="hyena_attention",
     )(
@@ -512,6 +591,16 @@
         jnp.asarray(forward), jnp.asarray(inverse),
         hyena_query, att_queries, att_keys,
     )
+    parts = 2
+    return pl.pallas_call(
+        functools.partial(copy_kernel, parts),
+        out_shape=outs,
+        in_specs=[anywhere] * 2,
+        out_specs=[anywhere] * 2,
+        scratch_shapes=[dma((2, parts))],
+        compiler_params=pltpu.CompilerParams(vmem_limit_bytes=60 * 1024 * 1024),
+        name="results",
+    )(hyena_out, attn_out)
 
 
 def by_shape(
@@ -520,6 +609,7 @@
     rows, channels = hyena_key.shape
     fits = (
         channels % (n * HD) == 0
+        and n % 2 == 0
         and rows % (2 * ABLK) == 0
         and rows // ABLK <= 8
         and block_mask.shape[1] <= 128

time: 105 us -> 153 us (1.46)
  Pallas kernels: 96.3 us -> 152 us
  local copies, waits for them, and re-layouts: 7.43 us -> 0 us
    pallas_call x1 -> x2, Pallas kernels: 96.3 us -> 152 us  [the longest x1 87.6 us: fused_on_device(): pl.pallas_call(functools.partial(fused_kernel, n, m), out_shape=outs, in_...]
    unnamed x16 -> x0, local copies, waits for them, and re-layouts: 7.43 us -> none
where the time goes in v2:
time: 153 us
  Pallas kernels  152 us (99%)
    pallas_call x1, Pallas kernels, fused_on_device(): pl.pallas_call(functools.partial(fused_kernel, n, m), out_shape=outs, in_...  87.6 us
    pallas_call x1, Pallas kernels, fused_on_device(): pl.pallas_call(functools.partial(copy_kernel, parts), out_shape=outs, in_...  64.7 us

profile of v2, /device:TPU:0, one launch (start us, length us, event | category | flops | bytes accessed | tf_op | source)
XLA Modules:
  0.0 152.9 jit_solution(281299650277541841)
XLA Ops:
  0.6 87.6 %hyena_attention.1 = (bf16[256,2048]{1,0:T(8,128)(2,1)}, bf16[256,2048]{1,0:T(8,128)(2,1)}) custom-call(bf16[256,2048]{1,0:T(8,128)(2,1)} %hk_far.1, bf16[256,2048]{1,0:T(8,128)(2,1)} %hv_far.1, f32[128,256]{1,0:T(8,128)} %fil_far.1, s32[8,1,256]{2,1,0:T(1,128)} %bitcast.2, f32[8,1,256]{2,1,0:T(1,128)} %bitcast.3, s32[2,16]{1,0:T(2,128)} %mask_far.1, ...), custom_call_target="tpu_custom_call" | custom-call | tf_op jit(solution)/shard_map/hyena_attention/pallas_call | solution.py:544
  88.3 64.7 %results.1 = (bf16[256,2048]{1,0:T(8,128)(2,1)}, bf16[256,2048]{1,0:T(8,128)(2,1)}) custom-call(bf16[256,2048]{1,0:T(8,128)(2,1)} %get-tuple-element.4.hy, bf16[256,2048]{1,0:T(8,128)(2,1)} %get-tuple-element.5.at), custom_call_target="tpu_custom_call" | custom-call | tf_op jit(solution)/shard_map/results/pallas_call | solution.py:595

commit v3 on v2

--- a/solution.py
+++ b/solution.py
@@ -452,13 +452,12 @@
 
     def attend(r):
 
-        def scores(h, k, add):
+        def scores(h, k):
             part = slice(h * HD, (h + 1) * HD)
-            raw = lax.dot_general(
+            return lax.dot_general(
                 query_in[r, :, part], key_in[k, :, part], (((1,), (1,)), ((), ())),
                 preferred_element_type=f32,
             )
-            return raw + add
 
         def weighted(h, k, weights):
             part = slice(h * HD, (h + 1) * HD)
@@ -475,22 +474,23 @@
         add = jnp.where(col <= row, added(r), -1e30)
         state = []
         for h in range(heads):
-            here = scores(h, r, add)
+            here = scores(h, r) + add
             top = jnp.max(here, axis=1, keepdims=True)
             weights = jnp.exp2((here - top) * scale)
-            state.append((top, lane_sum(weights), weighted(h, r, weights)))
+            state.append((top, lane_sum(weights), weighted(h, r, weights), scores(h, 0)))
 
         def step(k, state):
             add = added(k)
             out = []
             for h in range(heads):
-                top, total, acc = state[h]
-                here = scores(h, k, add)
+                top, total, acc, raw = state[h]
+                ahead = scores(h, k + 1)
+                here = raw + add
                 new_top = jnp.maximum(top, jnp.max(here, axis=1, keepdims=True))
                 weights = jnp.exp2((here - new_top) * scale)
                 keep = jnp.exp2((top - new_top) * scale)
                 total = total * keep + lane_sum(weights)
-                out.append((new_top, total, acc * keep + weighted(h, k, weights)))
+                out.append((new_top, total, acc * keep + weighted(h, k, weights), ahead))
             return tuple(out)
 
         state = lax.fori_loop(0, r, step, tuple(state))
@@ -515,16 +515,20 @@
         attn_copy(d).wait()
 
 
-def copy_kernel(parts, hy, at, hy_out, at_out, sems):
+def copy_kernel(parts, hy, at, hy_out, at_out, held, load, store):
     step = hy.shape[0] // parts
-    copies = []
+    loads, stores = [], []
     for i, (src, dst) in enumerate([(hy, hy_out), (at, at_out)]):
         for k in range(parts):
             part = pl.ds(k * step, step)
-            copies.append(pltpu.make_async_copy(src.at[part], dst.at[part], sems.at[i, k]))
-    for copy in copies:
+            loads.append(pltpu.make_async_copy(src.at[part], held.at[i, part], load.at[i, k]))
+            stores.append(pltpu.make_async_copy(held.at[i, part], dst.at[part], store.at[i, k]))
+    for copy in loads:
         copy.start()
-    for copy in copies:
+    for first, second in zip(loads, stores):
+        first.wait()
+        second.start()
+    for copy in stores:
         copy.wait()
 
 
@@ -591,13 +595,13 @@
         jnp.asarray(forward), jnp.asarray(inverse),
         hyena_query, att_queries, att_keys,
     )
-    parts = 2
+    parts = 4
     return pl.pallas_call(
         functools.partial(copy_kernel, parts),
         out_shape=outs,
         in_specs=[anywhere] * 2,
         out_specs=[anywhere] * 2,
-        scratch_shapes=[dma((2, parts))],
+        scratch_shapes=[pltpu.VMEM((2, rows, channels), bf16), dma((2, parts)), dma((2, parts))],
         compiler_params=pltpu.CompilerParams(vmem_limit_bytes=60 * 1024 * 1024),
         name="results",
     )(hyena_out, attn_out)

time: 153 us -> 84 us (0.55)
  Pallas kernels: 152 us -> 83.2 us
    pallas_call x1, Pallas kernels: 64.7 us -> 2.4 us  [fused_on_device(): pl.pallas_call(functools.partial(copy_kernel, parts), out_shape=outs, in_...]
    pallas_call x1, Pallas kernels: 87.6 us -> 80.8 us  [fused_on_device(): pl.pallas_call(functools.partial(fused_kernel, n, m), out_shape=outs, in_...]
where the time goes in v3:
time: 84 us; the launch traced here: 83.8 us
  Pallas kernels  83.2 us (99%)
    pallas_call x1, Pallas kernels, fused_on_device(): pl.pallas_call(functools.partial(fused_kernel, n, m), out_shape=outs, in_...  80.8 us
    pallas_call x1, Pallas kernels, fused_on_device(): pl.pallas_call(functools.partial(copy_kernel, parts), out_shape=outs, in_...  2.4 us

profile of v3, /device:TPU:0, one launch (start us, length us, event | category | flops | bytes accessed | tf_op | source)
XLA Modules:
  0.0 83.8 jit_solution(298777201069659744)
XLA Ops:
  0.6 80.8 %hyena_attention.1 = (bf16[256,2048]{1,0:T(8,128)(2,1)}, bf16[256,2048]{1,0:T(8,128)(2,1)}) custom-call(bf16[256,2048]{1,0:T(8,128)(2,1)} %hk_far.1, bf16[256,2048]{1,0:T(8,128)(2,1)} %hv_far.1, f32[128,256]{1,0:T(8,128)} %fil_far.1, s32[8,1,256]{2,1,0:T(1,128)} %bitcast.2, f32[8,1,256]{2,1,0:T(1,128)} %bitcast.3, s32[2,16]{1,0:T(2,128)} %mask_far.1, ...), custom_call_target="tpu_custom_call" | custom-call | tf_op jit(solution)/shard_map/hyena_attention/pallas_call | solution.py:548
  81.4 2.4 %results.1 = (bf16[256,2048]{1,0:T(8,128)(2,1)}, bf16[256,2048]{1,0:T(8,128)(2,1)}) custom-call(bf16[256,2048]{1,0:T(8,128)(2,1)} %get-tuple-element.4.hy, bf16[256,2048]{1,0:T(8,128)(2,1)} %get-tuple-element.5.at), custom_call_target="tpu_custom_call" | custom-call | tf_op jit(solution)/shard_map/results/pallas_call | solution.py:599

commit v4 on v3

--- a/solution.py
+++ b/solution.py
@@ -205,7 +205,7 @@
     hy, at,
     hk, hv, fil, grp, bias, mask, fwd, inv,
     mixed, select, bank, hot, masks, mixed_in, select_in, gate_in, query_in, key_in,
-    values, result, mask_add, spec, fspec,
+    values, result, mask_add, spec, fspec, scored, weighed, totals,
     lag_send, lag_recv, bank_send, bank_recv, pair_send, pair_recv, send, recv, local, loads,
 ):
     me = lax.axis_index("seq")
@@ -307,22 +307,23 @@
     bank[plane, pair] = fil[...].T.astype(bf16)
     masks[me] = jnp.zeros(masks.shape[1:], f32)
     masks[me, 0:subs, 0 : mask.shape[1]] = mask[...].astype(f32)
+    pl.semaphore_wait(barrier, n + m - 2)
+    for e in range(1, pairs):
+        lag_copy(e).start()
+    for d in range(1, m):
+        bank_copy(0, d).start()
+    for d in range(1, n):
+        mask_copy(d).start()
+    for d in range(1, n):
+        key_copy(d).start()
+    for d in range(1, n):
+        query_copy(d).start()
+
     near[2].wait()
     near[3].wait()
     for p in range(n):
         part = slice(p * wide, (p + 1) * wide)
         mixed[p] = (hk[:, part].astype(f32) * hv[:, part].astype(f32)).astype(bf16)
-
-    pl.semaphore_wait(barrier, n + m - 2)
-    for e in range(1, pairs):
-        lag_copy(e).start()
-    for d in range(1, m):
-        bank_copy(0, d).start()
-    for d in range(1, n):
-        mixed_copy(d).start()
-    for d in range(1, n):
-        mask_copy(d).start()
-
     mixed_in[me] = mixed[me]
     near[4].wait()
     lanes_here = bank.shape[3]
@@ -335,6 +336,88 @@
         for d in range(1, m):
             bank_copy(e, d).start()
 
+    for d in range(1, n):
+        mask_copy(d).wait()
+    flags = masks[...].reshape(n * masks.shape[1], masks.shape[2]).astype(bf16)
+    for k in range(n):
+        block_id = lax.broadcasted_iota(jnp.int32, (masks.shape[2], rows), 0)
+        owner = lax.broadcasted_iota(jnp.int32, (masks.shape[2], rows), 1) // ABLK + k * subs
+        spread = jnp.where(block_id == owner, 1.0, 0.0).astype(bf16)
+        shown = jnp.dot(flags, spread, preferred_element_type=f32)
+        mask_add[:, k] = ((shown - 1.0) * 1e30).reshape(n, masks.shape[1], rows)
+
+    own_in[1].wait()
+    own_in[2].wait()
+    for d in range(1, n):
+        key_copy(d).wait()
+    for d in range(1, n):
+        mixed_copy(d).start()
+    for d in range(1, n):
+        query_copy(d).wait()
+    for d in range(1, n):
+        gate_copy(d).start()
+    scale = HD ** (-0.5) / math.log(2.0)
+
+    def over_lanes(op, tile):
+        out = tile[:, 0:128]
+        for lane in range(128, rows, 128):
+            out = op(out, tile[:, lane : lane + 128])
+        return out
+
+    def weigh(r, carry):
+
+        def scores(h, k):
+            part = slice(h * HD, (h + 1) * HD)
+            return lax.dot_general(
+                query_in[r, :, part], key_in[k, :, part], (((1,), (1,)), ((), ())),
+                preferred_element_type=f32,
+            )
+
+        def added(k, more):
+            row_flags = mask_add[r, k] + more
+            return jnp.concatenate(
+                [jnp.broadcast_to(row_flags[i : i + 1], (ABLK, rows)) for i in range(subs)], axis=0
+            )
+
+        def score_pair(i, tops):
+            tops = list(tops)
+            for k in (2 * i, 2 * i + 1):
+                add = added(k, jnp.where(k < r, 0.0, -1e30).astype(f32))
+                for h in range(heads):
+                    here = scores(h, k) + add
+                    scored[k, h] = here
+                    tops[h] = jnp.maximum(tops[h], over_lanes(jnp.maximum, here))
+            return tuple(tops)
+
+        tops = lax.fori_loop(
+            0, (r + 1) // 2, score_pair, (jnp.full((rows, 128), -3e30, f32),) * heads
+        )
+        row = lax.broadcasted_iota(jnp.int32, (rows, rows), 0)
+        col = lax.broadcasted_iota(jnp.int32, (rows, rows), 1)
+        add = jnp.where(col <= row, added(r, 0.0), -1e30)
+        largest = []
+        for h in range(heads):
+            here = scores(h, r) + add
+            scored[r, h] = here
+            top = jnp.maximum(tops[h], over_lanes(jnp.maximum, here))
+            largest.append(jnp.max(top, axis=1, keepdims=True))
+
+        def weight(k, sums):
+            out = []
+            for h in range(heads):
+                weights = jnp.exp2((scored[k, h] - largest[h]) * scale)
+                weighed[r, k, h] = weights.astype(bf16)
+                out.append(sums[h] + over_lanes(jnp.add, weights))
+            return tuple(out)
+
+        sums = lax.fori_loop(0, r + 1, weight, (jnp.zeros((rows, 128), f32),) * heads)
+        for h in range(heads):
+            whole = jnp.sum(sums[h], axis=1, keepdims=True)
+            totals[r, h] = jnp.broadcast_to(whole, (rows, HD))
+        return carry
+
+    lax.fori_loop(0, n, weigh, 0)
+
     near[5].wait()
     spec[me] = jnp.dot(fwd[...], mixed_in[me], preferred_element_type=f32)
 
@@ -344,10 +427,7 @@
         spec[i] = jnp.dot(fwd[...], mixed_in[i], preferred_element_type=f32)
         return carry
 
-    lax.fori_loop(1, n // 2 + 1, signal_step, 0)
-    for d in range(1, n):
-        gate_copy(d).start()
-    lax.fori_loop(n // 2 + 1, n, signal_step, 0)
+    lax.fori_loop(1, n, signal_step, 0)
 
     def chosen(part, which):
         table = jnp.concatenate([bank[k, part] for k in range(m)], axis=1)
@@ -361,12 +441,6 @@
         pair_copy(e).start()
         own = 2 * part + side
         fspec[own] = jnp.dot(fwd[...], chosen(part, 0), preferred_element_type=f32)
-        if e == 0:
-            for d in range(1, n):
-                query_copy(d).start()
-        if e == min(1, pairs - 1):
-            for d in range(1, n):
-                key_copy(d).start()
     for e in range(pairs):
         pair_copy(e).wait()
         other = 2 * lax.rem(pair + pairs - e, pairs) + 1 - side
@@ -415,6 +489,7 @@
     def hyena_step(d, carry):
         gate_copy(n - d).wait()
         finish(lax.rem(me + d, n))
+        hyena_copy(d).start()
         return carry
 
     lax.fori_loop(1, n, hyena_step, 0)
@@ -422,81 +497,20 @@
     own_hyena = pltpu.make_async_copy(values.at[me], hy.at[:, columns(me)], local.at[3])
     own_hyena.start()
 
-    for d in range(1, n):
-        mask_copy(d).wait()
-    flags = masks[...].reshape(n * masks.shape[1], masks.shape[2]).astype(bf16)
-    for k in range(n):
-        block_id = lax.broadcasted_iota(jnp.int32, (masks.shape[2], rows), 0)
-        owner = lax.broadcasted_iota(jnp.int32, (masks.shape[2], rows), 1) // ABLK + k * subs
-        spread = jnp.where(block_id == owner, 1.0, 0.0).astype(bf16)
-        shown = jnp.dot(flags, spread, preferred_element_type=f32)
-        mask_add[:, k] = ((shown - 1.0) * 1e30).reshape(n, masks.shape[1], rows)
-
-    own_in[1].wait()
-    own_in[2].wait()
-    for d in range(1, n):
-        query_copy(d).wait()
-    for d in range(1, n // 2 + 1):
-        key_copy(d).wait()
-    for d in range(1, n):
-        hyena_copy(d).start()
-    for d in range(n // 2 + 1, n):
-        key_copy(d).wait()
-    scale = HD ** (-0.5) / math.log(2.0)
-
-    def lane_sum(weights):
-        total = weights[:, 0:128]
-        for lane in range(128, rows, 128):
-            total = total + weights[:, lane : lane + 128]
-        return total
-
     def attend(r):
 
-        def scores(h, k):
-            part = slice(h * HD, (h + 1) * HD)
-            return lax.dot_general(
-                query_in[r, :, part], key_in[k, :, part], (((1,), (1,)), ((), ())),
-                preferred_element_type=f32,
+        def step(k, accs):
+            return tuple(
+                accs[h] + jnp.dot(
+                    weighed[r, k, h], values[k, :, h * HD : (h + 1) * HD],
+                    preferred_element_type=f32,
+                )
+                for h in range(heads)
             )
 
-        def weighted(h, k, weights):
-            part = slice(h * HD, (h + 1) * HD)
-            return jnp.dot(weights.astype(bf16), values[k, :, part], preferred_element_type=f32)
-
-        def added(k):
-            flags_here = mask_add[r, k]
-            return jnp.concatenate(
-                [jnp.broadcast_to(flags_here[i : i + 1], (ABLK, rows)) for i in range(subs)], axis=0
-            )
-
-        row = lax.broadcasted_iota(jnp.int32, (rows, rows), 0)
-        col = lax.broadcasted_iota(jnp.int32, (rows, rows), 1)
-        add = jnp.where(col <= row, added(r), -1e30)
-        state = []
+        accs = lax.fori_loop(0, r + 1, step, (jnp.zeros((rows, HD), f32),) * heads)
         for h in range(heads):
-            here = scores(h, r) + add
-            top = jnp.max(here, axis=1, keepdims=True)
-            weights = jnp.exp2((here - top) * scale)
-            state.append((top, lane_sum(weights), weighted(h, r, weights), scores(h, 0)))
-
-        def step(k, state):
-            add = added(k)
-            out = []
-            for h in range(heads):
-                top, total, acc, raw = state[h]
-                ahead = scores(h, k + 1)
-                here = raw + add
-                new_top = jnp.maximum(top, jnp.max(here, axis=1, keepdims=True))
-                weights = jnp.exp2((here - new_top) * scale)
-                keep = jnp.exp2((top - new_top) * scale)
-                total = total * keep + lane_sum(weights)
-                out.append((new_top, total, acc * keep + weighted(h, k, weights), ahead))
-            return tuple(out)
-
-        state = lax.fori_loop(0, r, step, tuple(state))
-        for h in range(heads):
-            total = jnp.sum(state[h][1], axis=1, keepdims=True)
-            result[r, :, h * HD : (h + 1) * HD] = (state[h][2] / total).astype(bf16)
+            result[r, :, h * HD : (h + 1) * HD] = (accs[h] / totals[r, h]).astype(bf16)
 
     def attn_step(d, carry):
         attend(lax.rem(me + d, n))
@@ -574,6 +588,9 @@
             pltpu.VMEM((n, n, 8, rows), f32),
             pltpu.VMEM((n, 2 * rows, wide), f32),
             pltpu.VMEM((n, 2 * rows, wide), f32),
+            pltpu.VMEM((n, wide // HD, rows, rows), f32),
+            pltpu.VMEM((n, n, wide // HD, rows, rows), bf16),
+            pltpu.VMEM((n, wide // HD, rows, HD), f32),
             dma((pairs,)),
             dma((pairs,)),
             dma((pairs, m)),

time: 84 us -> 85.4 us (1.017)
  Pallas kernels: 83.2 us -> 84.4 us
    pallas_call x1, Pallas kernels: 80.8 us -> 82 us  [fused_on_device(): pl.pallas_call(functools.partial(fused_kernel, n, m), out_shape=outs, in_...]
where the time goes in v4:
time: 85.4 us; the launch traced here: 85.1 us
  Pallas kernels  84.4 us (99%)
    pallas_call x1, Pallas kernels, fused_on_device(): pl.pallas_call(functools.partial(fused_kernel, n, m), out_shape=outs, in_...  82 us
    pallas_call x1, Pallas kernels, fused_on_device(): pl.pallas_call(functools.partial(copy_kernel, parts), out_shape=outs, in_...  2.4 us

profile of v4, /device:TPU:0, one launch (start us, length us, event | category | flops | bytes accessed | tf_op | source)
XLA Modules:
  0.0 85.1 jit_solution(11855061598984049962)
XLA Ops:
  0.6 82.0 %hyena_attention.1 = (bf16[256,2048]{1,0:T(8,128)(2,1)}, bf16[256,2048]{1,0:T(8,128)(2,1)}) custom-call(bf16[256,2048]{1,0:T(8,128)(2,1)} %hk_far.1, bf16[256,2048]{1,0:T(8,128)(2,1)} %hv_far.1, f32[128,256]{1,0:T(8,128)} %fil_far.1, s32[8,1,256]{2,1,0:T(1,128)} %bitcast.2, f32[8,1,256]{2,1,0:T(1,128)} %bitcast.3, s32[2,16]{1,0:T(2,128)} %mask_far.1, ...), custom_call_target="tpu_custom_call" | custom-call | tf_op jit(solution)/shard_map/hyena_attention/pallas_call | solution.py:562
  82.7 2.4 %results.1 = (bf16[256,2048]{1,0:T(8,128)(2,1)}, bf16[256,2048]{1,0:T(8,128)(2,1)}) custom-call(bf16[256,2048]{1,0:T(8,128)(2,1)} %get-tuple-element.4.hy, bf16[256,2048]{1,0:T(8,128)(2,1)} %get-tuple-element.5.at), custom_call_target="tpu_custom_call" | custom-call | tf_op jit(solution)/shard_map/results/pallas_call | solution.py:616
